TPU v7x, 128 devices: a whole 4x4x4 slice. The times are simulated.
128 devices in a mesh: gx: 16 (over y, z_hi, core), gy: 8 (over x, z_lo).
Axes of the slice: x: 4, y: 4, z: 4 (z_hi: 2, z_lo: 2; z = z_hi * 2 + z_lo), core: 2. Of those that a mesh axis runs over, the one named last changes fastest.
Arguments:
- lam_start: float32 [64, 32, 1024], P(None, 'gx', 'gy'), may hold values from -6 to 6
- adj_rhs: float32 [64, 32, 1024], P(None, 'gx', 'gy'), may hold values from -6 to 6
- a_diag: bfloat16 [64, 64, 32, 1024], P(None, None, 'gx', 'gy')
- a_off: bfloat16 [4, 64, 64, 32, 1024], P(None, None, None, 'gx', 'gy'), may hold values from -0.119628906 to 0.119628906
- cols: int32 [4, 32, 1024], P(None, 'gx', 'gy'), may hold values from -1 to 32767, as said below
- smoother: bfloat16 [64, 64, 32, 1024], P(None, None, 'gx', 'gy')
- forward_u: float32 [64, 32, 1024], P(None, 'gx', 'gy'), may hold values from -6 to 6
- density: float32 [64, 32, 1024], P(None, 'gx', 'gy'), may hold values from 0.3 to 1
- owner_dev: int32 [16, 8, 256, 16], P('gx', 'gy'), may hold values from 0 to 127, all different within a row; in each aligned block of 256 rows (0 to 255, 256 to 511, ..., all dimensions but the last counted through in order) at most 64 rows name the same one
- owner_slot: int32 [16, 8, 256, 16], P('gx', 'gy'), may hold values from 0 to 255
- filt_weight: float32 [16, 8, 256, 16], P('gx', 'gy'), may hold values from 0.2 to 1
Outputs:
- adjoint: float32 [64, 32, 1024], P(None, 'gx', 'gy')
- filtered: float32 [64, 32, 1024], P(None, 'gx', 'gy')
Inputs may be any that keep to these rules, and one draw needn't show every extreme that they name: `cols`: for each block (x, y) the four entries are the indices x' * 1024 + y' of its four face neighbours (x +- 1, y), (x, y +- 1) in an order that varies from block to block, -1 for a neighbour beyond the grid's edge. `owner_dev`: each element block names 16 different ranks; the 256 element blocks of one device name any rank at most 64 times, a bound that some block reaches.
All inputs are finite; a program needn't handle non-finite values.
Results may differ from a plain program's by a relative error of at most 0.0003.
Values sent between devices are 32-bit elements; how exact they have to be, the bound alone decides.
A program may use at most 128 MiB of HBM per device.

v0:
```python
import jax
import jax.numpy as jnp
from jax import lax
from jax.experimental import pallas as pl
from jax.experimental.pallas import tpu as pltpu
from jax.sharding import PartitionSpec as P

SWEEPS = 3
F32 = jnp.float32
BF16 = jnp.bfloat16
MESH = pl.DeviceIdType.MESH
NN = (((1,), (0,)), ((), ()))


def merge4(accs, row):
    def step(p, q, mask, shift):
        return jnp.where(mask, p, q) + pltpu.roll(jnp.where(mask, q, p), shift, 0)

    low = (row % 4) < 2
    first = step(accs[0], accs[1], low, 6)
    second = step(accs[2], accs[3], low, 6)
    return step(first, second, row < 4, 4)


def matvec(pairs, write, group, unroll):
    row = lax.broadcasted_iota(jnp.int32, (8, 128), 0)

    def body(g, carry):
        accs = [None] * group
        for blocks, vector in pairs:
            for t in range(8):
                v = vector[16 * t : 16 * t + 16, :]
                for q in range(group):
                    p = blocks[g * group + q, 16 * t : 16 * t + 16, :].astype(F32) * v
                    accs[q] = p[:8] + p[8:] if accs[q] is None else (accs[q] + p[:8]) + p[8:]
        for h in range(group // 4):
            write(g * (group // 4) + h, merge4(accs[4 * h : 4 * h + 4], row))
        return carry

    lax.fori_loop(0, 64 // group, body, 0, unroll=unroll)


def eight(t):
    return pl.ds(pl.multiple_of(t * 8, 8), 8)


def kernel(
    lam_hbm, rhs_hbm, diag_hbm, off_hbm, cols_hbm, smooth_hbm, fu_hbm, dens_hbm, odev_hbm, oslot_hbm, fw_hbm,
    adj_out, filt_out,
    adj, rhs, diag, off, smooth, cols, fu, dens, odev, oslot, fw,
    res, nb, hxs, hxr, hys, hyr, own, route_send, route_near, route_far, far_in, onehot, xg, dens2, ps, pr, filt,
    in_sem, out_sem, hx_send, hx_recv, hy_send, hy_recv, rt_send, rt_recv, fr_sem, xg_send, xg_recv, xf_send, xf_recv,
    rs_send, rs_recv,
):
    ix = lax.axis_index("gx")
    iy = lax.axis_index("gy")
    half = ix // 2
    core = ix % 2
    partner = half * 2 + 1 - core

    def gy_peer(o):
        return (ix, lax.rem(iy + o, 8))

    def gx_peer(o):
        return (lax.rem(half + o, 8) * 2 + core, iy)

    right = lax.rem(ix + 1, 16)
    left = lax.rem(ix + 15, 16)

    sources = [
        (lam_hbm, adj), (odev_hbm, odev), (oslot_hbm, oslot), (fw_hbm, fw), (cols_hbm, cols), (rhs_hbm, rhs),
        (diag_hbm, diag), (off_hbm.at[0], off.at[0]), (off_hbm.at[1], off.at[1]), (off_hbm.at[2], off.at[2]),
        (off_hbm.at[3], off.at[3]), (smooth_hbm, smooth), (fu_hbm, fu), (dens_hbm, dens),
    ]
    loads = [pltpu.make_async_copy(a, b, in_sem.at[n]) for n, (a, b) in enumerate(sources)]
    for load in loads:
        load.start()

    barrier = pltpu.get_barrier_semaphore()
    for o in range(1, 8):
        pl.semaphore_signal(barrier, inc=1, device_id=gy_peer(o), device_id_type=MESH)
        pl.semaphore_signal(barrier, inc=1, device_id=gx_peer(o), device_id_type=MESH)
    for x in (right, left):
        pl.semaphore_signal(barrier, inc=1, device_id=(x, iy), device_id_type=MESH)

    row = lax.broadcasted_iota(jnp.int32, (8, 128), 0)
    lane = lax.broadcasted_iota(jnp.int32, (8, 128), 1)
    odd = (row % 2) == 1
    even = (row % 2) == 0

    def remote(src, dst, send, recv, device):
        return pltpu.make_async_remote_copy(
            src_ref=src, dst_ref=dst, send_sem=send, recv_sem=recv, device_id=device, device_id_type=MESH
        )

    def halo_copies(n):
        return [
            remote(hxs.at[n, 0], hxr.at[n, 0], hx_send.at[n, 0], hx_recv.at[n, 0], (right, iy)),
            remote(hxs.at[n, 1], hxr.at[n, 1], hx_send.at[n, 1], hx_recv.at[n, 1], (left, iy)),
            remote(hys.at[n, 0], hyr.at[n, 0], hy_send.at[n, 0], hy_recv.at[n, 0], gy_peer(1)),
            remote(hys.at[n, 1], hyr.at[n, 1], hy_send.at[n, 1], hy_recv.at[n, 1], gy_peer(7)),
        ]

    def halo_pack(n):
        up = jnp.zeros((8, 128), F32)
        down = jnp.zeros((8, 128), F32)
        for t in range(16):
            v = adj[8 * t : 8 * t + 8, :]
            up = jnp.where(lane == t, pltpu.roll(v, t + 1, 1), up)
            down = jnp.where(lane == t, pltpu.roll(v, t, 1) if t else v, down)
        hys[n, 0] = up
        hys[n, 1] = down
        for t in range(8):
            v, w = adj[8 * t : 8 * t + 8, :], adj[64 + 8 * t : 72 + 8 * t, :]
            hxs[n, 0, 8 * t : 8 * t + 8, :] = jnp.where(odd, v, pltpu.roll(w, 7, 0))
            hxs[n, 1, 8 * t : 8 * t + 8, :] = jnp.where(even, v, pltpu.roll(w, 1, 0))

    def neighbours(n):
        x = ix * 2 + row % 2
        y = iy * 128 + lane
        here = x * 1024 + y
        expects = [
            jnp.where(x >= 1, here - 1024, -5),
            jnp.where(x < 31, here + 1024, -5),
            jnp.where(y >= 1, here - 1, -5),
            jnp.where(y < 1023, here + 1, -5),
        ]
        named = [jnp.concatenate([cols[k]] * 4, axis=0) for k in range(4)]
        match = [[named[k] == e for e in expects] for k in range(4)]
        below, above = hyr[n, 0], hyr[n, 1]
        for t in range(16):
            v = adj[8 * t : 8 * t + 8, :]
            u = t % 8
            lo, hi = hxr[n, 0, 8 * u : 8 * u + 8, :], hxr[n, 1, 8 * u : 8 * u + 8, :]
            if t < 8:
                lo, hi = pltpu.roll(lo, 7, 0), pltpu.roll(hi, 1, 0)
            shifted = [
                jnp.where(even, lo, pltpu.roll(v, 1, 0)),
                jnp.where(odd, hi, pltpu.roll(v, 7, 0)),
                jnp.where(lane == 0, pltpu.roll(below, (128 - t) % 128, 1) if t else below, pltpu.roll(v, 1, 1)),
                jnp.where(lane == 127, pltpu.roll(above, 127 - t, 1), pltpu.roll(v, 127, 1)),
            ]
            for k in range(4):
                value = jnp.zeros((8, 128), F32)
                for m in range(4):
                    value = jnp.where(match[k][m], shifted[m], value)
                nb[k, 8 * t : 8 * t + 8, :] = value

    def routes(block, carry):
        far, oy = block // 8, block % 8
        to_core = core + far - 2 * core * far
        to_half = (half + lax.broadcasted_iota(jnp.int32, (8, 256), 0)) % 8
        rank = to_half * 16 + to_core * 8 + (iy + oy) % 8
        slot = jnp.full((8, 256), -1, jnp.int32)
        weight = jnp.zeros((8, 256), F32)
        for r in range(16):
            hit = odev[r : r + 1, :] == rank
            slot = jnp.where(hit, oslot[r : r + 1, :], slot)
            weight = jnp.where(hit, fw[r : r + 1, :], weight)
        route_send[far, oy, :8, :] = slot.astype(F32)
        route_send[far, oy, 8:, :] = weight
        return carry

    loads[0].wait()
    for n in (1, 2, 3):
        loads[n].wait()
    halo_pack(0)
    pl.semaphore_wait(barrier, 16)
    for copy in halo_copies(0):
        copy.start()
    lax.fori_loop(0, 16, routes, 0)
    route_near[0] = route_send[0, 0]
    route_far[0] = route_send[1, 0]

    def route_copies(o):
        return [
            remote(route_send.at[0, o], route_near.at[o], rt_send.at[0, o], rt_recv.at[0, o], gy_peer(o)),
            remote(route_send.at[1, o], route_far.at[o], rt_send.at[1, o], rt_recv.at[1, o], gy_peer(o)),
        ]

    for o in range(1, 8):
        for copy in route_copies(o):
            copy.start()
    route_forward = remote(route_far, far_in, fr_sem.at[0], fr_sem.at[1], (partner, iy))

    def start_residual(t, x):
        res[eight(t), :] = rhs[eight(t), :] - x

    def lower_residual(t, x):
        res[eight(t), :] = res[eight(t), :] - x

    def raise_adjoint(t, x):
        adj[eight(t), :] = adj[eight(t), :] + x

    column = lax.broadcasted_iota(jnp.int32, (256, 256), 1).astype(F32).astype(BF16)

    def build(table, base):
        def body(s, carry):
            slots = jnp.transpose(table[s, :8, :]).astype(BF16)
            for d in range(8):
                hit = jnp.broadcast_to(slots[:, d : d + 1], (256, 256)) == column
                onehot[base + s, d] = jnp.where(hit, BF16(1), BF16(0))
            return carry

        lax.fori_loop(0, 8, body, 0)

    for n in range(SWEEPS):
        if n:
            halo_pack(n)
            for copy in halo_copies(n):
                copy.start()
        else:
            loads[4].wait()
            loads[5].wait()
            loads[6].wait()
        matvec([(diag, adj)], start_residual, 8, 1)
        if n == 1:
            build(route_near, 0)
        if n == 2:
            build(far_in, 8)
        for copy in halo_copies(n):
            copy.wait_recv()
        neighbours(n)
        if n == 0:
            for k in range(4):
                loads[7 + k].wait()
                matvec([(off.at[k], nb.at[k])], lower_residual, 8, 1)
            loads[11].wait()
            for o in range(1, 8):
                for copy in route_copies(o):
                    copy.wait_recv()
            route_forward.start()
        else:
            matvec([(off.at[k], nb.at[k]) for k in range(4)], lower_residual, 4, 2)
        if n == 1:
            route_forward.wait_recv()
        matvec([(smooth, res)], raise_adjoint, 8, 1)

    loads[12].wait()
    loads[13].wait()
    adj_copy = pltpu.make_async_copy(adj, adj_out, out_sem.at[0])
    adj_copy.start()
    d = dens[...]
    own[...] = -3.0 * d * d * d * adj[...] * fu[...]
    for b in range(2):
        xg[0, :, 128 * b : 128 * b + 128] = own[pl.ds(b, 64, 2), :]
        dens2[:, 128 * b : 128 * b + 128] = dens[pl.ds(b, 64, 2), :]

    spread = {
        o: remote(xg.at[0], xg.at[o], xg_send.at[o], xg_recv.at[o], gy_peer(o)) for o in range(1, 8)
    }
    passed = [remote(xg.at[o], xg.at[8 + o], xf_send.at[o], xf_recv.at[o], (partner, iy)) for o in range(8)]
    for o in (4, 3, 5, 2, 6, 1, 7):
        spread[o].start()
    passed[0].start()
    for o in (1, 7, 2, 6, 3, 5, 4):
        spread[o].wait_recv()
        passed[o].start()
    for o in range(8):
        passed[o].wait_recv()

    def partial(d):
        acc = jnp.zeros((144, 256), F32)
        for s in range(16):
            table = route_near if s < 8 else far_in
            w = table[s % 8, pl.ds(8 + d, 1), :]
            p = xg[s] * w
            top = p.astype(BF16)
            rest = (p - top.astype(F32)).astype(BF16)
            w16 = jnp.broadcast_to(w, (16, 256))
            wtop = w16.astype(BF16).astype(F32)
            r16 = lax.broadcasted_iota(jnp.int32, (16, 256), 0)
            tail = jnp.where(r16 == 0, wtop, jnp.where(r16 == 1, w16 - wtop, 0.0)).astype(BF16)
            lhs = jnp.concatenate([top, rest, tail], axis=0)
            acc += lax.dot_general(lhs, onehot[s, d], NN, preferred_element_type=F32)
        weights = acc[128:136] + pltpu.roll(acc[128:136], 7, 0)
        return acc[:64] + acc[64:128], weights

    def reduce_copy(d):
        return remote(ps.at[d], pr.at[d], rs_send.at[d], rs_recv.at[d], gx_peer(d))

    def send_partial(d, carry):
        values, weights = partial(d)
        ps[d, :64] = values
        ps[d, 64:] = weights
        reduce_copy(d).start()
        return carry

    lax.fori_loop(1, 8, send_partial, 0)
    values, weights = partial(0)
    for d in range(1, 8):
        reduce_copy(d).wait_recv()
    for d in range(1, 8):
        values += pr[d, :64]
        weights += pr[d, 64:]
    total = weights[0:1]
    result = (xg[0] + values) / (dens2[...] * (1.0 + total))
    for b in range(2):
        filt[pl.ds(b, 64, 2), :] = result[:, 128 * b : 128 * b + 128]
    filt_copy = pltpu.make_async_copy(filt, filt_out, out_sem.at[1])
    filt_copy.start()

    for n in range(SWEEPS):
        for copy in halo_copies(n):
            copy.wait_send()
    for o in range(1, 8):
        for copy in route_copies(o):
            copy.wait_send()
        spread[o].wait_send()
        reduce_copy(o).wait_send()
    for copy in passed:
        copy.wait_send()
    route_forward.wait_send()
    adj_copy.wait()
    filt_copy.wait()


def local(lam_start, adj_rhs, a_diag, a_off, cols, smoother, forward_u, density, owner_dev, owner_slot, filt_weight):
    width, rows_x, rows_y = lam_start.shape
    rows = width * rows_x

    def by_row(x):
        return x.reshape(x.shape[:-3] + (rows, rows_y))

    def by_owner(x):
        return jnp.transpose(x, (0, 1, 3, 2)).reshape(x.shape[3], x.shape[2])

    any_spec = pl.BlockSpec(memory_space=pl.ANY)
    dma = pltpu.SemaphoreType.DMA
    vm = pltpu.VMEM
    adjoint, filtered = pl.pallas_call(
        kernel,
        out_shape=[jax.ShapeDtypeStruct((rows, rows_y), F32)] * 2,
        in_specs=[any_spec] * 11,
        out_specs=[any_spec] * 2,
        scratch_shapes=[
            vm((128, 128), F32), vm((128, 128), F32), vm((64, 128, 128), BF16), vm((4, 64, 128, 128), BF16),
            vm((64, 128, 128), BF16), vm((4, 2, 128), jnp.int32), vm((128, 128), F32), vm((128, 128), F32),
            vm((16, 256), jnp.int32), vm((16, 256), jnp.int32), vm((16, 256), F32),
            vm((128, 128), F32), vm((4, 128, 128), F32), vm((3, 2, 64, 128), F32), vm((3, 2, 64, 128), F32),
            vm((3, 2, 8, 128), F32), vm((3, 2, 8, 128), F32), vm((128, 128), F32),
            vm((2, 8, 16, 256), F32), vm((8, 16, 256), F32), vm((8, 16, 256), F32), vm((8, 16, 256), F32),
            vm((16, 8, 256, 256), BF16), vm((16, 64, 256), F32), vm((64, 256), F32),
            vm((8, 72, 256), F32), vm((8, 72, 256), F32), vm((128, 128), F32),
            dma((14,)), dma((2,)), dma((3, 2)), dma((3, 2)), dma((3, 2)), dma((3, 2)), dma((2, 8)), dma((2, 8)),
            dma((2,)), dma((8,)), dma((8,)), dma((8,)), dma((8,)), dma((8,)), dma((8,)),
        ],
        compiler_params=pltpu.CompilerParams(
            collective_id=0, has_side_effects=True, vmem_limit_bytes=56 * 2**20
        ),
        name="sweeps_and_filter",
    )(
        by_row(lam_start), by_row(adj_rhs), by_row(a_diag), by_row(a_off), cols, by_row(smoother),
        by_row(forward_u), by_row(density), by_owner(owner_dev), by_owner(owner_slot), by_owner(filt_weight),
    )
    shape = (width, rows_x, rows_y)
    return adjoint.reshape(shape), filtered.reshape(shape)


def solution(mesh):
    in_specs = (
        P(None, "gx", "gy"),
        P(None, "gx", "gy"),
        P(None, None, "gx", "gy"),
        P(None, None, None, "gx", "gy"),
        P(None, "gx", "gy"),
        P(None, None, "gx", "gy"),
        P(None, "gx", "gy"),
        P(None, "gx", "gy"),
        P("gx", "gy", None, None),
        P("gx", "gy", None, None),
        P("gx", "gy", None, None),
    )
    out_specs = (P(None, "gx", "gy"), P(None, "gx", "gy"))
    return jax.shard_map(local, mesh=mesh, in_specs=in_specs, out_specs=out_specs, check_vma=False)
```

profile of v0, /device:TPU:1, one launch (start us, length us, event | category | flops | bytes accessed | tf_op | source)
XLA Modules:
  0.0 54.8 jit_solution(14149212943245715240)
XLA Ops:
  0.6 51.2 %sweeps_and_filter.1 = (f32[128,128]{1,0:T(8,128)}, f32[128,128]{1,0:T(8,128)}) custom-call(f32[128,128]{1,0:T(8,128)} %bitcast.21, f32[128,128]{1,0:T(8,128)} %bitcast.22, bf16[64,128,128]{2,1,0:T(8,128)(2,1)} %bitcast.19, bf16[4,64,128,128]{3,2,1,0:T(8,128)(2,1)} %bitcast.18, s32[4,2,128]{2,1,0:T(2,128)} %cols_hbm.1, bf16[64,128,128]{2,1,0:T(8,128)(2,1)} %bitcast.20, ...), custom_call_target="tpu_custom_call" | custom-call | tf_op jit(solution)/shard_map/sweeps_and_filter/pallas_call | solution.py:331
  51.8 1.5 %copy.15 = f32[64,2,128]{2,1,0:T(2,128)} copy(f32[64,2,128]{2,1,0:T(2,128)} %bitcast.26) | data formatting | bytes 131072
  53.3 1.5 %copy.16 = f32[64,2,128]{2,1,0:T(2,128)} copy(f32[64,2,128]{2,1,0:T(2,128)} %bitcast.25) | data formatting | bytes 131072
where the time goes:
time: 55 us; the launch traced here: 54.8 us
  Pallas kernels  51.2 us (93%)
  local copies, waits for them, and re-layouts  2.95 us (5%)
  between operations  0.64 us (1%)
    pallas_call x1, Pallas kernels, local(): pl.pallas_call(kernel, out_shape=[jax.ShapeDtypeStruct((rows, rows_y), F3...  51.2 us
    unnamed x2, local copies, waits for them, and re-layouts  2.95 us

commit v1 on v0

--- a/solution.py
+++ b/solution.py
@@ -10,6 +10,7 @@
 BF16 = jnp.bfloat16
 MESH = pl.DeviceIdType.MESH
 NN = (((1,), (0,)), ((), ()))
+AHEAD = 2
 
 
 def merge4(accs, row):
@@ -48,8 +49,8 @@
     lam_hbm, rhs_hbm, diag_hbm, off_hbm, cols_hbm, smooth_hbm, fu_hbm, dens_hbm, odev_hbm, oslot_hbm, fw_hbm,
     adj_out, filt_out,
     adj, rhs, diag, off, smooth, cols, fu, dens, odev, oslot, fw,
-    res, nb, hxs, hxr, hys, hyr, own, route_send, route_near, route_far, far_in, onehot, xg, dens2, ps, pr, filt,
-    in_sem, out_sem, hx_send, hx_recv, hy_send, hy_recv, rt_send, rt_recv, fr_sem, xg_send, xg_recv, xf_send, xf_recv,
+    res, nb, off_x, off_y, halo, hxs, hxr, hys, hyr, own, route_send, route_near, route_far, onehot, xg, dens2, factor, cs, cr, ps, pr, filt,
+    in_sem, out_sem, hx_send, hx_recv, hy_send, hy_recv, rt_send, rt_recv, xg_send, xg_recv, xc_send, xc_recv,
     rs_send, rs_recv,
 ):
     ix = lax.axis_index("gx")
@@ -101,7 +102,13 @@
             remote(hys.at[n, 1], hyr.at[n, 1], hy_send.at[n, 1], hy_recv.at[n, 1], gy_peer(7)),
         ]
 
-    def halo_pack(n):
+    def pack_x(n):
+        for t in range(8):
+            v, w = adj[8 * t : 8 * t + 8, :], adj[64 + 8 * t : 72 + 8 * t, :]
+            hxs[n, 0, 8 * t : 8 * t + 8, :] = jnp.where(odd, v, pltpu.roll(w, 7, 0))
+            hxs[n, 1, 8 * t : 8 * t + 8, :] = jnp.where(even, v, pltpu.roll(w, 1, 0))
+
+    def pack_y(n):
         up = jnp.zeros((8, 128), F32)
         down = jnp.zeros((8, 128), F32)
         for t in range(16):
@@ -110,12 +117,8 @@
             down = jnp.where(lane == t, pltpu.roll(v, t, 1) if t else v, down)
         hys[n, 0] = up
         hys[n, 1] = down
-        for t in range(8):
-            v, w = adj[8 * t : 8 * t + 8, :], adj[64 + 8 * t : 72 + 8 * t, :]
-            hxs[n, 0, 8 * t : 8 * t + 8, :] = jnp.where(odd, v, pltpu.roll(w, 7, 0))
-            hxs[n, 1, 8 * t : 8 * t + 8, :] = jnp.where(even, v, pltpu.roll(w, 1, 0))
-
-    def neighbours(n):
+
+    def matches():
         x = ix * 2 + row % 2
         y = iy * 128 + lane
         here = x * 1024 + y
@@ -126,25 +129,57 @@
             jnp.where(y < 1023, here + 1, -5),
         ]
         named = [jnp.concatenate([cols[k]] * 4, axis=0) for k in range(4)]
-        match = [[named[k] == e for e in expects] for k in range(4)]
+        return [[named[k] == e for e in expects] for k in range(4)]
+
+    def inner_neighbours():
+        match = matches()
+        zero = jnp.zeros((8, 128), F32)
+        keep = [odd, even, lane > 0, lane < 127]
+        masks = [[match[k][m] & keep[m] for m in range(4)] for k in range(4)]
+        for t in range(16):
+            v = adj[8 * t : 8 * t + 8, :]
+            shifted = [pltpu.roll(v, 1, 0), pltpu.roll(v, 7, 0), pltpu.roll(v, 1, 1), pltpu.roll(v, 127, 1)]
+            for k in range(4):
+                value = zero
+                for m in range(4):
+                    value = jnp.where(masks[k][m], shifted[m], value)
+                nb[k, 8 * t : 8 * t + 8, :] = value
+
+    def gather_outer():
+        match = matches()
+        none = jnp.full((8, 128), 9.0, F32)
+        along_x, along_y = none, none
+        for k in range(4):
+            along_x = jnp.where((even & match[k][0]) | (odd & match[k][1]), float(k), along_x)
+            first, last = match[k][2] & (lane == 0), match[k][3] & (lane == 127)
+            along_y = jnp.where(first | last, float(k), along_y)
+        pick_x = jnp.concatenate([along_x] * 2, axis=0).astype(BF16)
+        pick_y = jnp.concatenate([along_y] * 2, axis=0).astype(BF16)
+
+        def body(i, carry):
+            for t in range(8):
+                rows = slice(16 * t, 16 * t + 16)
+                a = [off[k, i, rows, :] for k in range(4)]
+                for pick, out in ((pick_x, off_x), (pick_y, off_y)):
+                    value = jnp.zeros((16, 128), BF16)
+                    for k in range(4):
+                        value = jnp.where(pick == BF16(k), a[k], value)
+                    out[i, rows, :] = value
+            return carry
+
+        lax.fori_loop(0, 64, body, 0)
+
+    def outer_x(n):
+        for t in range(8):
+            lo, hi = hxr[n, 0, 8 * t : 8 * t + 8, :], hxr[n, 1, 8 * t : 8 * t + 8, :]
+            halo[8 * t : 8 * t + 8, :] = jnp.where(even, pltpu.roll(lo, 7, 0), pltpu.roll(hi, 1, 0))
+            halo[64 + 8 * t : 72 + 8 * t, :] = jnp.where(even, lo, hi)
+
+    def outer_y(n):
         below, above = hyr[n, 0], hyr[n, 1]
         for t in range(16):
-            v = adj[8 * t : 8 * t + 8, :]
-            u = t % 8
-            lo, hi = hxr[n, 0, 8 * u : 8 * u + 8, :], hxr[n, 1, 8 * u : 8 * u + 8, :]
-            if t < 8:
-                lo, hi = pltpu.roll(lo, 7, 0), pltpu.roll(hi, 1, 0)
-            shifted = [
-                jnp.where(even, lo, pltpu.roll(v, 1, 0)),
-                jnp.where(odd, hi, pltpu.roll(v, 7, 0)),
-                jnp.where(lane == 0, pltpu.roll(below, (128 - t) % 128, 1) if t else below, pltpu.roll(v, 1, 1)),
-                jnp.where(lane == 127, pltpu.roll(above, 127 - t, 1), pltpu.roll(v, 127, 1)),
-            ]
-            for k in range(4):
-                value = jnp.zeros((8, 128), F32)
-                for m in range(4):
-                    value = jnp.where(match[k][m], shifted[m], value)
-                nb[k, 8 * t : 8 * t + 8, :] = value
+            lo = pltpu.roll(below, 128 - t, 1) if t else below
+            halo[8 * t : 8 * t + 8, :] = jnp.where(lane == 0, lo, pltpu.roll(above, 127 - t, 1))
 
     def routes(block, carry):
         far, oy = block // 8, block % 8
@@ -161,16 +196,6 @@
         route_send[far, oy, 8:, :] = weight
         return carry
 
-    loads[0].wait()
-    for n in (1, 2, 3):
-        loads[n].wait()
-    halo_pack(0)
-    pl.semaphore_wait(barrier, 16)
-    for copy in halo_copies(0):
-        copy.start()
-    lax.fori_loop(0, 16, routes, 0)
-    route_near[0] = route_send[0, 0]
-    route_far[0] = route_send[1, 0]
 
     def route_copies(o):
         return [
@@ -178,11 +203,6 @@
             remote(route_send.at[1, o], route_far.at[o], rt_send.at[1, o], rt_recv.at[1, o], gy_peer(o)),
         ]
 
-    for o in range(1, 8):
-        for copy in route_copies(o):
-            copy.start()
-    route_forward = remote(route_far, far_in, fr_sem.at[0], fr_sem.at[1], (partner, iy))
-
     def start_residual(t, x):
         res[eight(t), :] = rhs[eight(t), :] - x
 
@@ -191,6 +211,9 @@
 
     def raise_adjoint(t, x):
         adj[eight(t), :] = adj[eight(t), :] + x
+
+    def inner_off():
+        matvec([(off.at[k], nb.at[k]) for k in range(4)], lower_residual, 4, 2)
 
     column = lax.broadcasted_iota(jnp.int32, (256, 256), 1).astype(F32).astype(BF16)
 
@@ -204,67 +227,82 @@
 
         lax.fori_loop(0, 8, body, 0)
 
+    loads[0].wait()
+    pack_x(0)
+    pack_y(0)
+    for n in (1, 2, 3):
+        loads[n].wait()
+    lax.fori_loop(0, 16, routes, 0)
+    route_near[0] = route_send[0, 0]
+    route_far[0] = route_send[1, 0]
+    pl.semaphore_wait(barrier, 16)
+    for copy in halo_copies(0):
+        copy.start()
+    for n in (4, 5, 6):
+        loads[n].wait()
+    matvec([(diag, adj)], start_residual, 8, 1)
+    inner_neighbours()
+    for k in range(4):
+        loads[7 + k].wait()
+    gather_outer()
+    inner_off()
+    loads[11].wait()
+    loads[12].wait()
+    loads[13].wait()
+    d = dens[...]
+    factor[...] = -3.0 * d * d * d * fu[...]
+    for b in range(2):
+        dens2[:, 128 * b : 128 * b + 128] = dens[pl.ds(b, 64, 2), :]
+
     for n in range(SWEEPS):
+        copies = halo_copies(n)
         if n:
-            halo_pack(n)
-            for copy in halo_copies(n):
-                copy.start()
-        else:
-            loads[4].wait()
-            loads[5].wait()
-            loads[6].wait()
-        matvec([(diag, adj)], start_residual, 8, 1)
-        if n == 1:
-            build(route_near, 0)
-        if n == 2:
-            build(far_in, 8)
-        for copy in halo_copies(n):
-            copy.wait_recv()
-        neighbours(n)
+            pack_x(n)
+            copies[0].start()
+            copies[1].start()
+            pack_y(n)
+            copies[2].start()
+            copies[3].start()
+            matvec([(diag, adj)], start_residual, 8, 1)
+            inner_neighbours()
+            inner_off()
+        copies[2].wait_recv()
+        copies[3].wait_recv()
+        outer_y(n)
+        matvec([(off_y, halo)], lower_residual, 8, 1)
+        copies[0].wait_recv()
+        copies[1].wait_recv()
         if n == 0:
-            for k in range(4):
-                loads[7 + k].wait()
-                matvec([(off.at[k], nb.at[k])], lower_residual, 8, 1)
-            loads[11].wait()
             for o in range(1, 8):
                 for copy in route_copies(o):
-                    copy.wait_recv()
-            route_forward.start()
-        else:
-            matvec([(off.at[k], nb.at[k]) for k in range(4)], lower_residual, 4, 2)
-        if n == 1:
-            route_forward.wait_recv()
+                    copy.start()
+        outer_x(n)
+        matvec([(off_x, halo)], lower_residual, 8, 1)
         matvec([(smooth, res)], raise_adjoint, 8, 1)
 
-    loads[12].wait()
-    loads[13].wait()
     adj_copy = pltpu.make_async_copy(adj, adj_out, out_sem.at[0])
     adj_copy.start()
-    d = dens[...]
-    own[...] = -3.0 * d * d * d * adj[...] * fu[...]
+    own[...] = factor[...] * adj[...]
     for b in range(2):
         xg[0, :, 128 * b : 128 * b + 128] = own[pl.ds(b, 64, 2), :]
-        dens2[:, 128 * b : 128 * b + 128] = dens[pl.ds(b, 64, 2), :]
 
     spread = {
         o: remote(xg.at[0], xg.at[o], xg_send.at[o], xg_recv.at[o], gy_peer(o)) for o in range(1, 8)
     }
-    passed = [remote(xg.at[o], xg.at[8 + o], xf_send.at[o], xf_recv.at[o], (partner, iy)) for o in range(8)]
-    for o in (4, 3, 5, 2, 6, 1, 7):
+    for o in (4, 3, 5, 1, 7, 2, 6):
         spread[o].start()
-    passed[0].start()
-    for o in (1, 7, 2, 6, 3, 5, 4):
-        spread[o].wait_recv()
-        passed[o].start()
-    for o in range(8):
-        passed[o].wait_recv()
-
-    def partial(d):
-        acc = jnp.zeros((144, 256), F32)
-        for s in range(16):
-            table = route_near if s < 8 else far_in
-            w = table[s % 8, pl.ds(8 + d, 1), :]
-            p = xg[s] * w
+    for o in range(1, 8):
+        for copy in route_copies(o):
+            copy.wait_recv()
+    build(route_far, 8)
+    build(route_near, 0)
+
+    def partial(far, d):
+        table = route_far if far else route_near
+        out = jnp.zeros((144, 256), F32)
+        for o in range(8):
+            w = table[o, pl.ds(8 + d, 1), :]
+            p = xg[o] * w
             top = p.astype(BF16)
             rest = (p - top.astype(F32)).astype(BF16)
             w16 = jnp.broadcast_to(w, (16, 256))
@@ -272,25 +310,49 @@
             r16 = lax.broadcasted_iota(jnp.int32, (16, 256), 0)
             tail = jnp.where(r16 == 0, wtop, jnp.where(r16 == 1, w16 - wtop, 0.0)).astype(BF16)
             lhs = jnp.concatenate([top, rest, tail], axis=0)
-            acc += lax.dot_general(lhs, onehot[s, d], NN, preferred_element_type=F32)
-        weights = acc[128:136] + pltpu.roll(acc[128:136], 7, 0)
-        return acc[:64] + acc[64:128], weights
+            out += lax.dot_general(lhs, onehot[8 * far + o, d], NN, preferred_element_type=F32)
+        return out[:64] + out[64:128], out[128:136] + pltpu.roll(out[128:136], 7, 0)
+
+    def cross_copy(d):
+        return remote(cs.at[d], cr.at[d], xc_send.at[d], xc_recv.at[d], (partner, iy))
 
     def reduce_copy(d):
         return remote(ps.at[d], pr.at[d], rs_send.at[d], rs_recv.at[d], gx_peer(d))
 
-    def send_partial(d, carry):
-        values, weights = partial(d)
-        ps[d, :64] = values
-        ps[d, 64:] = weights
+    def turn(k):
+        return (3 * k + 3) % 8
+
+    def send_cross(d):
+        values, weights = partial(1, d)
+        cs[d, :64] = values
+        cs[d, 64:] = weights
+        cross_copy(d).start()
+
+    def send_partial(k, carry):
+        d = turn(k)
+
+        @pl.when(k < 8 - AHEAD)
+        def _():
+            send_cross(turn(k + AHEAD))
+
+        values, weights = partial(0, d)
+        cross_copy(d).wait_recv()
+        ps[d, :64] = values + cr[d, :64]
+        ps[d, 64:] = weights + cr[d, 64:]
         reduce_copy(d).start()
         return carry
 
-    lax.fori_loop(1, 8, send_partial, 0)
-    values, weights = partial(0)
-    for d in range(1, 8):
+    for o in (2, 6, 1, 7, 4, 3, 5):
+        spread[o].wait_recv()
+    for k in range(AHEAD):
+        send_cross(turn(k))
+    lax.fori_loop(0, 7, send_partial, 0)
+    values, weights = partial(0, 0)
+    cross_copy(0).wait_recv()
+    values += cr[0, :64]
+    weights += cr[0, 64:]
+    for d in (2, 6, 4, 1, 7, 3, 5):
         reduce_copy(d).wait_recv()
-    for d in range(1, 8):
         values += pr[d, :64]
         weights += pr[d, 64:]
     total = weights[0:1]
@@ -308,11 +370,15 @@
             copy.wait_send()
         spread[o].wait_send()
         reduce_copy(o).wait_send()
-    for copy in passed:
-        copy.wait_send()
-    route_forward.wait_send()
+    for d in range(8):
+        cross_copy(d).wait_send()
     adj_copy.wait()
     filt_copy.wait()
+
+
+def hand_over(a, b, a_out, b_out):
+    a_out[...] = a[...]
+    b_out[...] = b[...]
 
 
 def local(lam_start, adj_rhs, a_diag, a_off, cols, smoother, forward_u, density, owner_dev, owner_slot, filt_weight):
@@ -337,13 +403,15 @@
             vm((128, 128), F32), vm((128, 128), F32), vm((64, 128, 128), BF16), vm((4, 64, 128, 128), BF16),
             vm((64, 128, 128), BF16), vm((4, 2, 128), jnp.int32), vm((128, 128), F32), vm((128, 128), F32),
             vm((16, 256), jnp.int32), vm((16, 256), jnp.int32), vm((16, 256), F32),
-            vm((128, 128), F32), vm((4, 128, 128), F32), vm((3, 2, 64, 128), F32), vm((3, 2, 64, 128), F32),
+            vm((128, 128), F32), vm((4, 128, 128), F32), vm((64, 128, 128), BF16), vm((64, 128, 128), BF16),
+            vm((128, 128), F32), vm((3, 2, 64, 128), F32), vm((3, 2, 64, 128), F32),
             vm((3, 2, 8, 128), F32), vm((3, 2, 8, 128), F32), vm((128, 128), F32),
-            vm((2, 8, 16, 256), F32), vm((8, 16, 256), F32), vm((8, 16, 256), F32), vm((8, 16, 256), F32),
-            vm((16, 8, 256, 256), BF16), vm((16, 64, 256), F32), vm((64, 256), F32),
+            vm((2, 8, 16, 256), F32), vm((8, 16, 256), F32), vm((8, 16, 256), F32),
+            vm((16, 8, 256, 256), BF16), vm((8, 64, 256), F32), vm((64, 256), F32), vm((128, 128), F32),
+            vm((8, 72, 256), F32), vm((8, 72, 256), F32),
             vm((8, 72, 256), F32), vm((8, 72, 256), F32), vm((128, 128), F32),
             dma((14,)), dma((2,)), dma((3, 2)), dma((3, 2)), dma((3, 2)), dma((3, 2)), dma((2, 8)), dma((2, 8)),
-            dma((2,)), dma((8,)), dma((8,)), dma((8,)), dma((8,)), dma((8,)), dma((8,)),
+            dma((8,)), dma((8,)), dma((8,)), dma((8,)), dma((8,)), dma((8,)),
         ],
         compiler_params=pltpu.CompilerParams(
             collective_id=0, has_side_effects=True, vmem_limit_bytes=56 * 2**20
@@ -353,6 +421,13 @@
         by_row(lam_start), by_row(adj_rhs), by_row(a_diag), by_row(a_off), cols, by_row(smoother),
         by_row(forward_u), by_row(density), by_owner(owner_dev), by_owner(owner_slot), by_owner(filt_weight),
     )
+    adjoint, filtered = pl.pallas_call(
+        hand_over,
+        out_shape=[jax.ShapeDtypeStruct((rows, rows_y), F32)] * 2,
+        in_specs=[pl.BlockSpec(memory_space=vm)] * 2,
+        out_specs=[pl.BlockSpec(memory_space=vm)] * 2,
+        name="hand_over",
+    )(adjoint, filtered)
     shape = (width, rows_x, rows_y)
     return adjoint.reshape(shape), filtered.reshape(shape)
 

time: 55 us -> 49.2 us (0.89)
  local copies, waits for them, and re-layouts: 2.95 us -> 0 us
  Pallas kernels: 51.2 us -> 48.4 us
    pallas_call x1, Pallas kernels: 51.2 us -> 46.9 us  [local(): pl.pallas_call(kernel, out_shape=[jax.ShapeDtypeStruct((rows, rows_y), F3...]
    unnamed x2 -> x0, local copies, waits for them, and re-layouts: 2.95 us -> none
    pallas_call x0 -> x1, Pallas kernels: none -> 1.53 us  [local(): pl.pallas_call(hand_over, out_shape=[jax.ShapeDtypeStruct((rows, rows_y),...]
where the time goes in v1:
time: 49.2 us; the launch traced here: 49 us
  Pallas kernels  48.4 us (98%)
  between operations  0.64 us (1%)
    pallas_call x1, Pallas kernels, local(): pl.pallas_call(kernel, out_shape=[jax.ShapeDtypeStruct((rows, rows_y), F3...  46.9 us
    pallas_call x1, Pallas kernels, local(): pl.pallas_call(hand_over, out_shape=[jax.ShapeDtypeStruct((rows, rows_y),...  1.53 us

profile of v1, /device:TPU:1, one launch (start us, length us, event | category | flops | bytes accessed | tf_op | source)
XLA Modules:
  0.0 49.0 jit_solution(14590567341120085957)
XLA Ops:
  0.6 46.9 %sweeps_and_filter.1 = (f32[128,128]{1,0:T(8,128)}, f32[128,128]{1,0:T(8,128)}) custom-call(f32[128,128]{1,0:T(8,128)} %bitcast.21, f32[128,128]{1,0:T(8,128)} %bitcast.22, bf16[64,128,128]{2,1,0:T(8,128)(2,1)} %bitcast.19, bf16[4,64,128,128]{3,2,1,0:T(8,128)(2,1)} %bitcast.18, s32[4,2,128]{2,1,0:T(2,128)} %cols_hbm.1, bf16[64,128,128]{2,1,0:T(8,128)(2,1)} %bitcast.20, ...), custom_call_target="tpu_custom_call" | custom-call | tf_op jit(solution)/shard_map/sweeps_and_filter/pallas_call | solution.py:397
  47.5 1.5 %hand_over.1 = (f32[128,128]{1,0:T(8,128)}, f32[128,128]{1,0:T(8,128)}) custom-call(f32[128,128]{1,0:T(8,128)} %get-tuple-element.6.a, f32[128,128]{1,0:T(8,128)} %get-tuple-element.7.b), custom_call_target="tpu_custom_call" | custom-call | tf_op jit(solution)/shard_map/hand_over/pallas_call | solution.py:424

commit v2 on v1

--- a/solution.py
+++ b/solution.py
@@ -1,3 +1,5 @@
+import functools
+
 import jax
 import jax.numpy as jnp
 from jax import lax
@@ -277,8 +279,8 @@
                 for copy in route_copies(o):
                     copy.start()
         outer_x(n)
-        matvec([(off_x, halo)], lower_residual, 8, 1)
-        matvec([(smooth, res)], raise_adjoint, 8, 1)
+        matvec([(off_x, halo)], lower_residual, 8, 2)
+        matvec([(smooth, res)], raise_adjoint, 8, 2)
 
     adj_copy = pltpu.make_async_copy(adj, adj_out, out_sem.at[0])
     adj_copy.start()
@@ -320,7 +322,7 @@
         return remote(ps.at[d], pr.at[d], rs_send.at[d], rs_recv.at[d], gx_peer(d))
 
     def turn(k):
-        return (3 * k + 3) % 8
+        return (2 * k + 3 - 9 * (k // 4)) % 8
 
     def send_cross(d):
         values, weights = partial(1, d)
@@ -328,13 +330,11 @@
         cs[d, 64:] = weights
         cross_copy(d).start()
 
-    def send_partial(k, carry):
+    def send_partial(k, carry, ahead):
         d = turn(k)
 
-        @pl.when(k < 8 - AHEAD)
-        def _():
+        if ahead:
             send_cross(turn(k + AHEAD))
-
         values, weights = partial(0, d)
         cross_copy(d).wait_recv()
         ps[d, :64] = values + cr[d, :64]
@@ -346,12 +346,13 @@
         spread[o].wait_recv()
     for k in range(AHEAD):
         send_cross(turn(k))
-    lax.fori_loop(0, 7, send_partial, 0)
+    lax.fori_loop(0, 8 - AHEAD, functools.partial(send_partial, ahead=True), 0, unroll=2)
+    lax.fori_loop(8 - AHEAD, 7, functools.partial(send_partial, ahead=False), 0)
     values, weights = partial(0, 0)
     cross_copy(0).wait_recv()
     values += cr[0, :64]
     weights += cr[0, 64:]
-    for d in (2, 6, 4, 1, 7, 3, 5):
+    for d in (2, 4, 6, 7, 1, 3, 5):
         reduce_copy(d).wait_recv()
         values += pr[d, :64]
         weights += pr[d, 64:]

time: 49.2 us -> 49.1 us (level)
  no operation moved by 1% of the time
where the time goes in v2:
time: 49.1 us; the launch traced here: 48.9 us
  Pallas kernels  48.3 us (98%)
  between operations  0.64 us (1%)
    pallas_call x1, Pallas kernels, local(): pl.pallas_call(kernel, out_shape=[jax.ShapeDtypeStruct((rows, rows_y), F3...  46.7 us
    pallas_call x1, Pallas kernels, local(): pl.pallas_call(hand_over, out_shape=[jax.ShapeDtypeStruct((rows, rows_y),...  1.53 us

profile of v2, /device:TPU:1, one launch (start us, length us, event | category | flops | bytes accessed | tf_op | source)
XLA Modules:
  0.0 48.9 jit_solution(17028649180342573676)
XLA Ops:
  0.6 46.7 %sweeps_and_filter.1 = (f32[128,128]{1,0:T(8,128)}, f32[128,128]{1,0:T(8,128)}) custom-call(f32[128,128]{1,0:T(8,128)} %bitcast.21, f32[128,128]{1,0:T(8,128)} %bitcast.22, bf16[64,128,128]{2,1,0:T(8,128)(2,1)} %bitcast.19, bf16[4,64,128,128]{3,2,1,0:T(8,128)(2,1)} %bitcast.18, s32[4,2,128]{2,1,0:T(2,128)} %cols_hbm.1, bf16[64,128,128]{2,1,0:T(8,128)(2,1)} %bitcast.20, ...), custom_call_target="tpu_custom_call" | custom-call | tf_op jit(solution)/shard_map/sweeps_and_filter/pallas_call | solution.py:398
  47.4 1.5 %hand_over.1 = (f32[128,128]{1,0:T(8,128)}, f32[128,128]{1,0:T(8,128)}) custom-call(f32[128,128]{1,0:T(8,128)} %get-tuple-element.6.a, f32[128,128]{1,0:T(8,128)} %get-tuple-element.7.b), custom_call_target="tpu_custom_call" | custom-call | tf_op jit(solution)/shard_map/hand_over/pallas_call | solution.py:425

commit v3 on v2

--- a/solution.py
+++ b/solution.py
@@ -291,7 +291,7 @@
     spread = {
         o: remote(xg.at[0], xg.at[o], xg_send.at[o], xg_recv.at[o], gy_peer(o)) for o in range(1, 8)
     }
-    for o in (4, 3, 5, 1, 7, 2, 6):
+    for o in (3, 5, 1, 7, 4, 2, 6):
         spread[o].start()
     for o in range(1, 8):
         for copy in route_copies(o):

time: 49.1 us -> 48.7 us (level)
  no operation moved by 1% of the time
where the time goes in v3:
time: 48.7 us; the launch traced here: 48.5 us
  Pallas kernels  47.9 us (98%)
  between operations  0.64 us (1%)
    pallas_call x1, Pallas kernels, local(): pl.pallas_call(kernel, out_shape=[jax.ShapeDtypeStruct((rows, rows_y), F3...  46.4 us
    pallas_call x1, Pallas kernels, local(): pl.pallas_call(hand_over, out_shape=[jax.ShapeDtypeStruct((rows, rows_y),...  1.53 us

profile of v3, /device:TPU:1, one launch (start us, length us, event | category | flops | bytes accessed | tf_op | source)
XLA Modules:
  0.0 48.5 jit_solution(7120012561117841953)
XLA Ops:
  0.6 46.4 %sweeps_and_filter.1 = (f32[128,128]{1,0:T(8,128)}, f32[128,128]{1,0:T(8,128)}) custom-call(f32[128,128]{1,0:T(8,128)} %bitcast.21, f32[128,128]{1,0:T(8,128)} %bitcast.22, bf16[64,128,128]{2,1,0:T(8,128)(2,1)} %bitcast.19, bf16[4,64,128,128]{3,2,1,0:T(8,128)(2,1)} %bitcast.18, s32[4,2,128]{2,1,0:T(2,128)} %cols_hbm.1, bf16[64,128,128]{2,1,0:T(8,128)(2,1)} %bitcast.20, ...), custom_call_target="tpu_custom_call" | custom-call | tf_op jit(solution)/shard_map/sweeps_and_filter/pallas_call | solution.py:398
  47.0 1.5 %hand_over.1 = (f32[128,128]{1,0:T(8,128)}, f32[128,128]{1,0:T(8,128)}) custom-call(f32[128,128]{1,0:T(8,128)} %get-tuple-element.6.a, f32[128,128]{1,0:T(8,128)} %get-tuple-element.7.b), custom_call_target="tpu_custom_call" | custom-call | tf_op jit(solution)/shard_map/hand_over/pallas_call | solution.py:425
